TPU v7x, 32 devices: a whole 2x2x4 slice. The times are simulated.
32 devices in a mesh: group: 2 (over x), ctx: 4 (over y, core), exp: 4 (over z).
Axes of the slice: x: 2, y: 2, z: 4, core: 2. Of those that a mesh axis runs over, the one named last changes fastest.
Arguments:
- queries: bfloat16 [1024, 1536], P(('group', 'ctx'), 'exp'), may hold values from -10.5 to 10.5
- keys: bfloat16 [1024, 512], P(('group', 'ctx'), 'exp'), may hold values from -4 to 4
- values: bfloat16 [1024, 512], P(('group', 'ctx'), 'exp'), may hold values from -6 to 6
- residual_in: bfloat16 [1024, 1536], P(('group', 'ctx', 'exp')), may hold values from -6 to 6
- doc_lengths: int32 [4], replicated, may hold values from 1 to 384, 1024 in all
- w_out: bfloat16 [1536, 1536], P('exp', 'group'), may hold values from -0.15625 to 0.15625
- norm_gain: float32 [1536], replicated, may hold values from 0.5 to 1.5
- router: bfloat16 [1536, 16], replicated, may hold values from -0.15625 to 0.15625
- expert_ids: int32 [1024, 6], P(('group', 'ctx', 'exp')), may hold values from 0 to 15, all different within a row; in each aligned block of 32 rows (0 to 31, 32 to 63, ...) at most 18 rows name the same one
- expert_gate_up: bfloat16 [16, 1536, 1024], P(('ctx', 'exp'), 'group'), may hold values from -0.15625 to 0.15625
- expert_down: bfloat16 [16, 1536, 512], P(('ctx', 'exp'), 'group'), may hold values from -0.25 to 0.25
- shared_gate_up: bfloat16 [1536, 2, 1024], P(None, None, 'exp'), may hold values from -0.15625 to 0.15625
- shared_down: bfloat16 [1024, 1536], P('exp'), may hold values from -0.1875 to 0.1875
Outputs:
- hidden_out: bfloat16 [1024, 1536], P(('group', 'ctx', 'exp'))
Inputs may be any that keep to these rules, and one draw needn't show every extreme that they name: `doc_lengths`: documents are packed back to back in stream order and one of them has length 384. `expert_ids`: within the 32 rows of one device along group+ctx+exp, no expert is named by more than 18 routes, a bound that some block reaches.
All inputs are finite; a program needn't handle non-finite values.
Results may differ from a plain program's by a relative error of at most 0.015.
Values may be sent and summed in bfloat16 or wider, within the bound.
A program may use at most 64 MiB of HBM per device.

v0:
```python
import math
import jax
import jax.numpy as jnp
from jax import lax
from jax.sharding import PartitionSpec as P

HEAD = 128
neg_big = -1e30


def passed_along(shard, axis, by):
    length = lax.axis_size(axis)
    pairs = [(i, i + by) for i in range(length) if 0 <= i + by < length]
    return lax.ppermute(shard, axis, pairs)


def doc_starts(positions, doc_lengths):
    order = jnp.arange(doc_lengths.shape[0], dtype=jnp.int32)
    before = (order[None, :] <= order[:, None]).astype(jnp.int32)
    doc_ends = jnp.sum(before * doc_lengths[None, :], axis=1, dtype=jnp.int32)
    passed = (doc_ends[None, :] <= positions[:, None]).astype(jnp.int32)
    return jnp.sum(passed * doc_lengths[None, :], axis=1, dtype=jnp.int32)


def attend_block(soft_state, kv_block, source, query_heads, query_pos, query_start):
    run_max, run_sum, run_acc = soft_state
    rows_dev = kv_block.shape[1]
    key_pos = source * rows_dev + jnp.arange(rows_dev, dtype=jnp.int32)
    allowed = (key_pos[None, :] <= query_pos[:, None]) & (key_pos[None, :] >= query_start[:, None])
    key_heads = kv_block[0].reshape(rows_dev, -1, HEAD)
    value_heads = kv_block[1].reshape(rows_dev, -1, HEAD)
    scores = jnp.einsum(
        "tgpd,sgd->gpts", query_heads, key_heads, preferred_element_type=jnp.float32
    ) * (1.0 / math.sqrt(HEAD))
    scores = jnp.where(allowed, scores, neg_big)
    new_max = jnp.maximum(run_max, jnp.max(scores, axis=-1))
    weights = jnp.where(allowed, jnp.exp(scores - new_max[..., None]), 0.0)
    factor = jnp.exp(run_max - new_max)
    run_sum = run_sum * factor + jnp.sum(weights, axis=-1)
    run_acc = run_acc * factor[..., None] + jnp.einsum(
        "gpts,sgd->gptd",
        weights.astype(jnp.bfloat16),
        value_heads,
        preferred_element_type=jnp.float32,
    )
    return (new_max, run_sum, run_acc)


def visit_block(soft_state, kv_block, source, query_heads, query_pos, query_start):
    rows_dev = kv_block.shape[1]
    useful = (source >= 0) & (source * rows_dev + rows_dev - 1 >= query_start[0])

    def run_block(inner_state):
        return attend_block(inner_state, kv_block, source, query_heads, query_pos, query_start)

    def keep_block(inner_state):
        return inner_state

    return lax.cond(useful, run_block, keep_block, soft_state)


def turned(shard, axis, by):
    length = lax.axis_size(axis)
    return lax.ppermute(shard, axis, [(i, (i + by) % length) for i in range(length)])


def swapped(shard):
    return lax.ppermute(shard, "group", [(0, 1), (1, 0)])


def matmul(rows, weights):
    return jnp.dot(rows, weights, preferred_element_type=jnp.float32).astype(jnp.bfloat16)


def joined(own_first, own, other):
    first = jnp.where(own_first, own, other)
    second = jnp.where(own_first, other, own)
    return jnp.concatenate([first, second], axis=-1)


def summed_from(partial, length, rows, step):
    total = partial[:rows].astype(jnp.float32)
    for by in range(1, length):
        piece = partial[by * rows : (by + 1) * rows]
        total = total + turned(piece, "exp", step * by).astype(jnp.float32)
    return total


def attend_window(kv, first_key, query_heads, query_pos, query_start):
    count = kv.shape[1]
    key_pos = first_key + jnp.arange(count, dtype=jnp.int32)
    allowed = (key_pos[None, :] <= query_pos[:, None]) & (key_pos[None, :] >= query_start[:, None])
    key_heads = kv[0].reshape(count, -1, HEAD)
    value_heads = kv[1].reshape(count, -1, HEAD)
    scores = jnp.einsum(
        "tgpd,sgd->gpts", query_heads, key_heads, preferred_element_type=jnp.float32
    ) * (1.0 / math.sqrt(HEAD))
    scores = jnp.where(allowed, scores, neg_big)
    weights = jnp.where(allowed, jnp.exp(scores - jnp.max(scores, axis=-1, keepdims=True)), 0.0)
    acc = jnp.einsum(
        "gpts,sgd->gptd",
        weights.astype(jnp.bfloat16),
        value_heads,
        preferred_element_type=jnp.float32,
    )
    return acc / jnp.sum(weights, axis=-1, keepdims=True)


def on_device(
    queries,
    keys,
    values,
    residual_in,
    doc_lengths,
    w_out,
    norm_gain,
    router,
    expert_ids,
    expert_gate_up,
    expert_down,
    shared_gate_up,
    shared_down,
):
    rows_dev = queries.shape[0]
    kv_count = keys.shape[1] // HEAD
    per_kv = queries.shape[1] // HEAD // kv_count
    block_count = lax.axis_size("group") * lax.axis_size("ctx")
    look_back = min(32, block_count // 2)
    my_block = lax.axis_index("group") * lax.axis_size("ctx") + lax.axis_index("ctx")
    query_pos = my_block * rows_dev + jnp.arange(rows_dev, dtype=jnp.int32)
    query_start = doc_starts(query_pos, doc_lengths)
    query_heads = queries.reshape(rows_dev, kv_count, per_kv, HEAD)
    init_state = (
        jnp.full((kv_count, per_kv, rows_dev), neg_big, jnp.float32),
        jnp.zeros((kv_count, per_kv, rows_dev), jnp.float32),
        jnp.zeros((kv_count, per_kv, rows_dev, HEAD), jnp.float32),
    )
    group_size = lax.axis_size("group")
    swap = group_size == 2
    kv_own = jnp.stack([keys, values])
    if look_back <= 8:
        blocks = [passed_along(kv_own, ("group", "ctx"), by) for by in range(look_back - 1, 0, -1)]
        kv_all = jnp.concatenate([*blocks, kv_own], axis=1)
    if swap:
        out_other, gate_other, down_other = (
            swapped(w_out),
            swapped(expert_gate_up),
            swapped(expert_down),
        )
        own_first = lax.axis_index("group") == 0
    if look_back <= 8:
        first_key = (my_block - (look_back - 1)) * rows_dev
        attended = attend_window(kv_all, first_key, query_heads, query_pos, query_start)
    else:
        soft_state = visit_block(init_state, kv_own, my_block, query_heads, query_pos, query_start)

        def cycle_turn(turn_idx, loop_state):
            moving, inner_state = loop_state
            moving = passed_along(moving, ("group", "ctx"), 1)
            return (
                moving,
                visit_block(
                    inner_state, moving, my_block - turn_idx, query_heads, query_pos, query_start
                ),
            )

        moving, soft_state = lax.fori_loop(1, look_back, cycle_turn, (kv_own, soft_state))
        run_max, run_sum, run_acc = soft_state
        attended = run_acc / run_sum[..., None]
    attended = jnp.transpose(attended, (2, 0, 1, 3)).reshape(rows_dev, -1).astype(jnp.bfloat16)
    exp_size = lax.axis_size("exp")
    exp_me = lax.axis_index("exp")
    tok_e = rows_dev // exp_size
    ahead = [(exp_me + by) % exp_size for by in range(exp_size)]
    rolled = jnp.concatenate(
        [lax.dynamic_slice_in_dim(attended, to * tok_e, tok_e, 0) for to in ahead], axis=0
    )
    if swap:
        partial = joined(own_first, matmul(rolled, w_out), matmul(rolled, out_other))
    else:
        partial = matmul(rolled, lax.all_gather(w_out, "group", axis=1, tiled=True))
    projected = summed_from(partial, exp_size, tok_e, 1)
    stream = (residual_in.astype(jnp.float32) + projected).astype(jnp.bfloat16)
    stream_f = stream.astype(jnp.float32)
    normed = (
        stream_f
        * lax.rsqrt(jnp.mean(stream_f * stream_f, axis=-1, keepdims=True) + 1e-05)
        * norm_gain
    ).astype(jnp.bfloat16)
    expert_count = router.shape[1]
    route_count = expert_ids.shape[1]
    logits = jnp.dot(normed, router, preferred_element_type=jnp.float32)
    chosen = expert_ids[:, :, None] == jnp.arange(expert_count, dtype=jnp.int32)[None, None, :]
    picked_logits = jnp.sum(jnp.where(chosen, logits[:, None, :], 0.0), axis=-1)
    raw_gates = jax.nn.sigmoid(picked_logits)
    gate_probs = raw_gates / jnp.sum(raw_gates, axis=-1, keepdims=True)
    all_normed = jnp.concatenate(
        [normed, *[turned(normed, "exp", by) for by in range(1, exp_size)]], axis=0
    )
    shared_pre = jnp.einsum(
        "td,dkf->tkf", all_normed, shared_gate_up, preferred_element_type=jnp.float32
    )
    shared_act = (jax.nn.silu(shared_pre[:, 0]) * shared_pre[:, 1]).astype(jnp.bfloat16)
    shared_out = summed_from(matmul(shared_act, shared_down), exp_size, tok_e, -1)
    slot_count = max(2, 3 * tok_e * route_count // (2 * expert_count))
    flat_ids = expert_ids.reshape(-1)
    order = jnp.arange(flat_ids.shape[0], dtype=jnp.int32)
    earlier = (flat_ids[None, :] == flat_ids[:, None]) & (order[None, :] < order[:, None])
    slot_of = jnp.sum(earlier.astype(jnp.int32), axis=1, dtype=jnp.int32)
    target = flat_ids * slot_count + slot_of
    placing = (
        jnp.arange(expert_count * slot_count, dtype=jnp.int32)[:, None] == target[None, :]
    ).astype(jnp.bfloat16)
    placing = jnp.sum(placing.reshape(expert_count * slot_count, tok_e, route_count), axis=2)
    model_width = normed.shape[1]
    outgoing = (
        jnp.dot(placing, normed, preferred_element_type=jnp.float32)
        .astype(jnp.bfloat16)
        .reshape(expert_count, slot_count, model_width)
    )
    if not swap:
        gate_up_full = lax.all_gather(expert_gate_up, "group", axis=1, tiled=True)
        down_full = lax.all_gather(expert_down, "group", axis=1, tiled=True)
    hidden_count = expert_down.shape[2]
    local_experts = expert_gate_up.shape[0]
    arrived = lax.all_to_all(outgoing, ("ctx", "exp"), split_axis=0, concat_axis=0, tiled=True)
    sources = arrived.shape[0] // local_experts
    grouped = arrived.reshape(sources, local_experts, arrived.shape[1], arrived.shape[2])
    if swap:
        half = model_width // 2
        mine = lax.dynamic_slice_in_dim(grouped, lax.axis_index("group") * half, half, 3)
        others = lax.dynamic_slice_in_dim(grouped, (1 - lax.axis_index("group")) * half, half, 3)
        pre_act = jnp.einsum(
            "nekd,edf->nekf", mine, expert_gate_up, preferred_element_type=jnp.float32
        ) + jnp.einsum("nekd,edf->nekf", others, gate_other, preferred_element_type=jnp.float32)
    else:
        pre_act = jnp.einsum(
            "nekd,edf->nekf", grouped, gate_up_full, preferred_element_type=jnp.float32
        )
    activated = (jax.nn.silu(pre_act[..., :hidden_count]) * pre_act[..., hidden_count:]).astype(
        jnp.bfloat16
    )

    def down(rows):
        return jnp.einsum(
            "nekf,edf->nekd", activated, rows, preferred_element_type=jnp.float32
        ).astype(jnp.bfloat16)

    if swap:
        result = joined(own_first, down(expert_down), down(down_other))
    else:
        result = down(down_full)
    returned = lax.all_to_all(
        result.reshape(arrived.shape), ("ctx", "exp"), split_axis=0, concat_axis=0, tiled=True
    )
    flat_back = returned.reshape(expert_count * slot_count, model_width)
    fetched = (
        jnp.take(flat_back, target, axis=0)
        .reshape(tok_e, route_count, model_width)
        .astype(jnp.float32)
    )
    routed = jnp.sum(gate_probs[:, :, None] * fetched, axis=1)
    return (stream_f + shared_out + routed).astype(jnp.bfloat16)


def solution(mesh):
    in_specs = (
        P(("group", "ctx"), "exp"),
        P(("group", "ctx"), "exp"),
        P(("group", "ctx"), "exp"),
        P(("group", "ctx", "exp"), None),
        P(),
        P("exp", "group"),
        P(),
        P(),
        P(("group", "ctx", "exp"), None),
        P(("ctx", "exp"), "group", None),
        P(("ctx", "exp"), "group", None),
        P(None, None, "exp"),
        P("exp", None),
    )
    out_specs = P(("group", "ctx", "exp"), None)
    return jax.shard_map(
        on_device, mesh=mesh, in_specs=in_specs, out_specs=out_specs, check_vma=False
    )
```

profile of v0, /device:TPU:0, one launch (start us, length us, event | category | flops | bytes accessed | tf_op | source)
XLA Modules:
  0.0 148.1 jit_solution(8046579092838463045)
XLA Ops:
  0.0 0.9 pad_maximum_fusion.2
  0.9 2.3 %collective-permute-start.2 = (bf16[2,128,128]{2,1,0:T(8,128)(2,1)S(1)}, bf16[2,128,128]{2,1,0:T(8,128)(2,1)S(1)}, u32[]{:S(2)}, u32[]{:S(2)}) collective-permute-start(bf16[2,128,128]{2,1,0:T(8,128)(2,1)S(1)} %pad_maximum_fusion.2), channel_id=1, source_target_pairs={{0,4},{4,8},{8,12},{12,16},{16,20},{20,24},{24,28},{1,5},{5,9},{9,... | collective-permute-start | bytes 196616 | tf_op jit(solution)/shard_map/ppermute | solution.py:14
  3.3 4.4 %collective-permute-start.1 = (bf16[2,128,128]{2,1,0:T(8,128)(2,1)S(1)}, bf16[2,128,128]{2,1,0:T(8,128)(2,1)S(1)}, u32[]{:S(2)}, u32[]{:S(2)}) collective-permute-start(bf16[2,128,128]{2,1,0:T(8,128)(2,1)S(1)} %pad_maximum_fusion.2), channel_id=1, source_target_pairs={{0,8},{4,12},{8,16},{12,20},{16,24},{20,28},{1,9},{5,13},{9,17},{1... | collective-permute-start | bytes 196616 | tf_op jit(solution)/shard_map/ppermute | solution.py:14
  7.7 4.3 %collective-permute-start = (bf16[2,128,128]{2,1,0:T(8,128)(2,1)S(1)}, bf16[2,128,128]{2,1,0:T(8,128)(2,1)S(1)}, u32[]{:S(2)}, u32[]{:S(2)}) collective-permute-start(bf16[2,128,128]{2,1,0:T(8,128)(2,1)S(1)} %pad_maximum_fusion.2), channel_id=1, source_target_pairs={{0,12},{4,16},{8,20},{12,24},{16,28},{1,13},{5,17},{9,21},{13,25},... | collective-permute-start | bytes 196616 | tf_op jit(solution)/shard_map/ppermute | solution.py:14
  12.1 0.8 copy.37
  13.3 0.8 select_reduce_fusion.2
  14.1 0.7 select_reduce_fusion.1
  14.9 0.6 compare_and_fusion.1
  15.6 1.0 copy.31
  16.7 0.8 maximum_maximum_fusion
  17.9 0.3 fusion.10
  18.6 0.4 copy-done.2
  19.0 0.3 convolution_convert_fusion.5
  19.3 7.4 %collective-permute-done.3 = bf16[384,768]{1,0:T(8,128)(2,1)S(1)} collective-permute-done((bf16[384,768]{1,0:T(8,128)(2,1)}, bf16[384,768]{1,0:T(8,128)(2,1)S(1)}, u32[]{:S(2)}, u32[]{:S(2)}) %collective-permute-start.3) | collective-permute-done | bytes 589856 | tf_op jit(solution)/shard_map/ppermute | solution.py:68
  26.7 0.3 broadcast_select_fusion.1
  27.1 3.7 %collective-permute-start.6 = (bf16[32,1536]{1,0:T(8,128)(2,1)S(1)}, bf16[32,1536]{1,0:T(8,128)(2,1)S(1)}, u32[]{:S(2)}, u32[]{:S(2)}) collective-permute-start(bf16[32,1536]{1,0:T(8,128)(2,1)S(1)} %get-tuple-element.15), channel_id=1, source_target_pairs={{0,3},{1,0},{2,1},{3,2},{4,7},{5,4},{6,5},{7,6},{8,11},{9,8},{10,9... | collective-permute-start | bytes 294920 | tf_op jit(solution)/shard_map/ppermute | solution.py:64
  30.7 1.0 collective-permute-start.4
  31.8 1.5 %collective-permute-done.6 = bf16[32,1536]{1,0:T(8,128)(2,1)S(1)} collective-permute-done((bf16[32,1536]{1,0:T(8,128)(2,1)S(1)}, bf16[32,1536]{1,0:T(8,128)(2,1)S(1)}, u32[]{:S(2)}, u32[]{:S(2)}) %collective-permute-start.6) | collective-permute-done | bytes 98336 | tf_op jit(solution)/shard_map/ppermute | solution.py:64
  33.4 5.1 %collective-permute-done.5 = bf16[32,1536]{1,0:T(8,128)(2,1)S(1)} collective-permute-done((bf16[32,1536]{1,0:T(8,128)(2,1)S(1)}, bf16[32,1536]{1,0:T(8,128)(2,1)S(1)}, u32[]{:S(2)}, u32[]{:S(2)}) %collective-permute-start.5) | collective-permute-done | bytes 98336 | tf_op jit(solution)/shard_map/ppermute | solution.py:64
  38.8 0.4 convolution_convert_fusion
  39.2 1.3 reshape.190
  40.5 4.7 %all-to-all-start = ((bf16[16,18,1536]{2,1,0:T(8,128)(2,1)}), bf16[16,18,1536]{2,1,0:T(8,128)(2,1)S(1)}, u32[]{:S(2)}, u32[]{:S(2)}) async-start(bf16[16,18,1536]{2,1,0:T(8,128)(2,1)} %reshape.190), calls=%async_computation | async-start | bytes 2359296 | tf_op jit(solution)/shard_map/all_to_all | solution.py:226
  45.2 1.8 %collective-permute-start.13 = (bf16[1,768,1024]{2,1,0:T(8,128)(2,1)}, bf16[1,768,1024]{2,1,0:T(8,128)(2,1)}, u32[]{:S(2)}, u32[]{:S(2)}) collective-permute-start(bf16[1,768,1024]{2,1,0:T(8,128)(2,1)} %param.22), channel_id=1, source_target_pairs={{0,16},{16,0},{1,17},{17,1},{2,18},{18,2},{3,19},{19,3},{4,20},{20... | collective-permute-start | bytes 4718600 | tf_op jit(solution)/shard_map/ppermute | solution.py:68
  47.0 0.3 collective-permute-start.14
  47.4 0.6 pad_clamp_fusion
  48.0 3.7 %collective-permute-start.9 = (bf16[32,1536]{1,0:T(8,128)(2,1)S(1)}, bf16[32,1536]{1,0:T(8,128)(2,1)S(1)}, u32[]{:S(2)}, u32[]{:S(2)}) collective-permute-start(bf16[32,1536]{1,0:T(8,128)(2,1)S(1)} %fusion.34), channel_id=1, source_target_pairs={{0,3},{1,0},{2,1},{3,2},{4,7},{5,4},{6,5},{7,6},{8,11},{9,8},{10,9... | collective-permute-start | bytes 294920 | tf_op jit(solution)/shard_map/ppermute | solution.py:64
  51.7 1.1 collective-permute-start.7
  52.8 26.4 %all-to-all-done = bf16[16,18,1536]{2,1,0:T(8,128)(2,1)S(1)} async-done(((bf16[16,18,1536]{2,1,0:T(8,128)(2,1)}), bf16[16,18,1536]{2,1,0:T(8,128)(2,1)S(1)}, u32[]{:S(2)}, u32[]{:S(2)}) %all-to-all-start) | async-done | bytes 884768 | tf_op jit(solution)/shard_map/all_to_all | solution.py:226
  79.2 2.2 %fusion.2 = f32[16,18,1024]{2,1,0:T(8,128)S(1)} fusion(bf16[1,768,1024]{2,1,0:T(8,128)(2,1)} %param.22, bf16[16,18,1536]{2,1,0:T(8,128)(2,1)S(1)} %all-to-all-done, s32[]{:T(128)S(6)} %select_n.128), kind=kOutput, calls=%fused_computation.5 | convolution fusion | flops 452984832 | bytes 3342340 | tf_op jit(solution)/shard_map/nekd,edf->nekf/dot_general | solution.py:233
  81.4 1.4 collective-permute-done.13
  82.8 2.2 %add_bitcast_fusion = f32[16,1,18,1024]{3,2,0,1:T(8,128)S(1)} fusion(f32[16,18,1024]{2,1,0:T(8,128)S(1)} %fusion.2, bf16[1,768,1024]{2,1,0:T(8,128)(2,1)} %collective-permute-done.13, bf16[16,18,1536]{2,1,0:T(8,128)(2,1)S(1)} %all-to-all-done, s32[]{:T(128)S(6)} %select_n.129), kind=kOutput, calls=%fused_computation.10 | convolution fusion | flops 453279744 | bytes 4915204 | tf_op jit(solution)/shard_map/nekd,edf->nekf/dot_general | solution.py:235
  85.3 0.9 copy-done.1
  86.1 0.5 convolution_convert_fusion.3
  86.7 12.4 %collective-permute-done.14 = bf16[1,768,512]{2,1,0:T(8,128)(2,1)} collective-permute-done((bf16[1,768,512]{2,1,0:T(8,128)(2,1)}, bf16[1,768,512]{2,1,0:T(8,128)(2,1)}, u32[]{:S(2)}, u32[]{:S(2)}) %collective-permute-start.14) | collective-permute-done | bytes 786464 | tf_op jit(solution)/shard_map/ppermute | solution.py:68
  99.1 1.6 %select_bitcast_fusion.1 = (bf16[16,1,18,768]{3,2,0,1:T(8,128)(2,1)S(1)}, bf16[16,1,18,768]{3,2,0,1:T(8,128)(2,1)S(1)}) fusion(bf16[16,18,768]{2,1,0:T(8,128)(2,1)S(1)} %convolution_convert_fusion.3, pred[]{:T(512)S(6)} %eq.48, bf16[1,768,512]{2,1,0:T(8,128)(2,1)} %collective-permute-done.14, bf16[16,1,18,512]{3,2,0,1:T(8,128)(2,1)S(1)} %fusion.11), kind=kOutput, calls=%fused_computation.29 | convolution fusion | flops 227155968 | bytes 2408449 | tf_op jit(solution)/shard_map/nekf,edf->nekd/dot_general | solution.py:245
  100.7 1.1 maximum_bitcast_fusion
  101.8 5.9 %all-to-all-start.1 = ((bf16[16,18,1536]{2,1,0:T(8,128)(2,1)}), bf16[16,18,1536]{2,1,0:T(8,128)(2,1)}, u32[]{:S(2)}, u32[]{:S(2)}) async-start(bf16[16,18,1536]{2,1,0:T(8,128)(2,1)} %maximum_bitcast_fusion), calls=%async_computation.1 | async-start | bytes 2359296 | tf_op jit(solution)/shard_map/all_to_all | solution.py:253
  108.1 0.4 fusion.4
  108.5 0.7 copy-done.7
  109.5 0.7 fusion.53
  110.2 1.9 %collective-permute-start.12 = (bf16[32,1536]{1,0:T(8,128)(2,1)}, bf16[32,1536]{1,0:T(8,128)(2,1)}, u32[]{:S(2)}, u32[]{:S(2)}) collective-permute-start(bf16[32,1536]{1,0:T(8,128)(2,1)} %get-tuple-element.12), channel_id=1, source_target_pairs={{0,1},{1,2},{2,3},{3,0},{4,5},{5,6},{6,7},{7,4},{8,9},{9,10},{10,1... | collective-permute-start | bytes 294920 | tf_op jit(solution)/shard_map/ppermute | solution.py:64
  112.1 2.4 %collective-permute-start.11 = (bf16[32,1536]{1,0:T(8,128)(2,1)}, bf16[32,1536]{1,0:T(8,128)(2,1)}, u32[]{:S(2)}, u32[]{:S(2)}) collective-permute-start(bf16[32,1536]{1,0:T(8,128)(2,1)} %get-tuple-element.13), channel_id=1, source_target_pairs={{0,2},{1,3},{2,0},{3,1},{4,6},{5,7},{6,4},{7,5},{8,10},{9,11},{10,... | collective-permute-start | bytes 294920 | tf_op jit(solution)/shard_map/ppermute | solution.py:64
  114.5 1.5 collective-permute-start.10
  115.9 25.9 %all-to-all-done.1 = bf16[16,18,1536]{2,1,0:T(8,128)(2,1)} async-done(((bf16[16,18,1536]{2,1,0:T(8,128)(2,1)}), bf16[16,18,1536]{2,1,0:T(8,128)(2,1)}, u32[]{:S(2)}, u32[]{:S(2)}) %all-to-all-start.1) | async-done | bytes 884768 | tf_op jit(solution)/shard_map/all_to_all | solution.py:253
  141.8 1.5 %reshape.197 = bf16[288,1536]{1,0:T(8,128)(2,1)S(1)} reshape(bf16[16,18,1536]{2,1,0:T(8,128)(2,1)} %all-to-all-done.1) | data formatting | bytes 1769472 | tf_op jit(solution)/shard_map/reshape | solution.py:256
  143.3 1.2 gather_fusion
  144.7 1.6 %multiply_reduce_fusion = f32[32,1536]{1,0:T(8,128)S(1)} fusion(bf16[32,6,1536]{2,1,0:T(8,128)(2,1)S(1)} %gather.7, f32[32,6]{1,0:T(8,128)S(1)} %copy.36, pred[32,6]{1,0:T(8,128)(4,1)} %get-tuple-element.5), kind=kLoop, calls=%fused_computation.9 | loop fusion | flops 1130496 | bytes 787392 | tf_op jit(solution)/shard_map/reduce_sum | solution.py:262
  146.4 1.7 %fusion.36 = bf16[32,1536]{1,0:T(8,128)(2,1)} fusion(f32[32,1536]{1,0:T(8,128)S(1)} %multiply_reduce_fusion, bf16[32,1536]{1,0:T(8,128)(2,1)S(1)} %get-tuple-element.8, bf16[32,1536]{1,0:T(8,128)(2,1)} %collective-permute-done.12, bf16[32,1536]{1,0:T(8,128)(2,1)} %collective-permute-done.11, bf16[32,1536]{1,0:T(8,128)(2,1)} %collective-permute-done.10, ...), kind=kLoop, calls=%fused_computation.62 | loop fusion | flops 540672 | bytes 786432 | tf_op jit(solution)/shard_map/convert_element_type | solution.py:263
  (53 shorter events, 3.0 us)
Async XLA Ops:
  0.0 108.1 %copy-start = (bf16[1536,2,256]{2,1,0:T(2,128)(2,1)S(1)}, bf16[1536,2,256]{2,1,0:T(2,128)(2,1)}, u32[]{:S(2)}) copy-start(bf16[1536,2,256]{2,1,0:T(2,128)(2,1)} %param.24) | copy-start | bytes 4718596
  0.9 15.8 %collective-permute-start.2 = (bf16[2,128,128]{2,1,0:T(8,128)(2,1)S(1)}, bf16[2,128,128]{2,1,0:T(8,128)(2,1)S(1)}, u32[]{:S(2)}, u32[]{:S(2)}) collective-permute-start(bf16[2,128,128]{2,1,0:T(8,128)(2,1)S(1)} %pad_maximum_fusion.2), channel_id=1, source_target_pairs={{0,4},{4,8},{8,12},{12,16},{16,20},{20,24},{24,28},{1,5},{5,9},{9,... | collective-permute-start | bytes 196616 | tf_op jit(solution)/shard_map/ppermute | solution.py:14
  3.3 13.4 %collective-permute-start.1 = (bf16[2,128,128]{2,1,0:T(8,128)(2,1)S(1)}, bf16[2,128,128]{2,1,0:T(8,128)(2,1)S(1)}, u32[]{:S(2)}, u32[]{:S(2)}) collective-permute-start(bf16[2,128,128]{2,1,0:T(8,128)(2,1)S(1)} %pad_maximum_fusion.2), channel_id=1, source_target_pairs={{0,8},{4,12},{8,16},{12,20},{16,24},{20,28},{1,9},{5,13},{9,17},{1... | collective-permute-start | bytes 196616 | tf_op jit(solution)/shard_map/ppermute | solution.py:14
  7.7 9.0 %collective-permute-start = (bf16[2,128,128]{2,1,0:T(8,128)(2,1)S(1)}, bf16[2,128,128]{2,1,0:T(8,128)(2,1)S(1)}, u32[]{:S(2)}, u32[]{:S(2)}) collective-permute-start(bf16[2,128,128]{2,1,0:T(8,128)(2,1)S(1)} %pad_maximum_fusion.2), channel_id=1, source_target_pairs={{0,12},{4,16},{8,20},{12,24},{16,28},{1,13},{5,17},{9,21},{13,25},... | collective-permute-start | bytes 196616 | tf_op jit(solution)/shard_map/ppermute | solution.py:14
  12.0 14.7 %collective-permute-start.3 = (bf16[384,768]{1,0:T(8,128)(2,1)}, bf16[384,768]{1,0:T(8,128)(2,1)S(1)}, u32[]{:S(2)}, u32[]{:S(2)}) collective-permute-start(bf16[384,768]{1,0:T(8,128)(2,1)} %param.18), channel_id=1, source_target_pairs={{0,16},{16,0},{1,17},{17,1},{2,18},{18,2},{3,19},{19,3},{4,20},{20... | collective-permute-start | bytes 1769480 | tf_op jit(solution)/shard_map/ppermute | solution.py:68
  17.9 1.1 copy-start.2
  18.4 20.0 %copy-start.3 = (bf16[32,1536]{1,0:T(8,128)(2,1)S(1)}, bf16[32,1536]{1,0:T(8,128)(2,1)}, u32[]{:S(2)}) copy-start(bf16[32,1536]{1,0:T(8,128)(2,1)} %param.16) | copy-start | bytes 294916
  19.3 19.4 %copy-start.6 = (f32[1536]{0:T(1024)S(1)}, f32[1536]{0:T(1024)}, u32[]{:S(2)}) copy-start(f32[1536]{0:T(1024)} %param.19) | copy-start | bytes 18436
  27.1 6.3 %collective-permute-start.6 = (bf16[32,1536]{1,0:T(8,128)(2,1)S(1)}, bf16[32,1536]{1,0:T(8,128)(2,1)S(1)}, u32[]{:S(2)}, u32[]{:S(2)}) collective-permute-start(bf16[32,1536]{1,0:T(8,128)(2,1)S(1)} %get-tuple-element.15), channel_id=1, source_target_pairs={{0,3},{1,0},{2,1},{3,2},{4,7},{5,4},{6,5},{7,6},{8,11},{9,8},{10,9... | collective-permute-start | bytes 294920 | tf_op jit(solution)/shard_map/ppermute | solution.py:64
  30.7 7.7 %collective-permute-start.5 = (bf16[32,1536]{1,0:T(8,128)(2,1)S(1)}, bf16[32,1536]{1,0:T(8,128)(2,1)S(1)}, u32[]{:S(2)}, u32[]{:S(2)}) collective-permute-start(bf16[32,1536]{1,0:T(8,128)(2,1)S(1)} %get-tuple-element.16), channel_id=1, source_target_pairs={{0,2},{1,3},{2,0},{3,1},{4,6},{5,7},{6,4},{7,5},{8,10},{9,11},{10,... | collective-permute-start | bytes 294920 | tf_op jit(solution)/shard_map/ppermute | solution.py:64
  30.7 7.7 %collective-permute-start.4 = (bf16[32,1536]{1,0:T(8,128)(2,1)S(1)}, bf16[32,1536]{1,0:T(8,128)(2,1)S(1)}, u32[]{:S(2)}, u32[]{:S(2)}) collective-permute-start(bf16[32,1536]{1,0:T(8,128)(2,1)S(1)} %get-tuple-element.14), channel_id=1, source_target_pairs={{0,1},{1,2},{2,3},{3,0},{4,5},{5,6},{6,7},{7,4},{8,9},{9,10},{10,1... | collective-permute-start | bytes 294920 | tf_op jit(solution)/shard_map/ppermute | solution.py:64
  40.5 38.7 %all-to-all-start = ((bf16[16,18,1536]{2,1,0:T(8,128)(2,1)}), bf16[16,18,1536]{2,1,0:T(8,128)(2,1)S(1)}, u32[]{:S(2)}, u32[]{:S(2)}) async-start(bf16[16,18,1536]{2,1,0:T(8,128)(2,1)} %reshape.190), calls=%async_computation | async-start | bytes 2359296 | tf_op jit(solution)/shard_map/all_to_all | solution.py:226
  45.2 37.6 %collective-permute-start.13 = (bf16[1,768,1024]{2,1,0:T(8,128)(2,1)}, bf16[1,768,1024]{2,1,0:T(8,128)(2,1)}, u32[]{:S(2)}, u32[]{:S(2)}) collective-permute-start(bf16[1,768,1024]{2,1,0:T(8,128)(2,1)} %param.22), channel_id=1, source_target_pairs={{0,16},{16,0},{1,17},{17,1},{2,18},{18,2},{3,19},{19,3},{4,20},{20... | collective-permute-start | bytes 4718600 | tf_op jit(solution)/shard_map/ppermute | solution.py:68
  47.0 52.1 %collective-permute-start.14 = (bf16[1,768,512]{2,1,0:T(8,128)(2,1)}, bf16[1,768,512]{2,1,0:T(8,128)(2,1)}, u32[]{:S(2)}, u32[]{:S(2)}) collective-permute-start(bf16[1,768,512]{2,1,0:T(8,128)(2,1)} %param.23), channel_id=1, source_target_pairs={{0,16},{16,0},{1,17},{17,1},{2,18},{18,2},{3,19},{19,3},{4,20},{20... | collective-permute-start | bytes 2359304 | tf_op jit(solution)/shard_map/ppermute | solution.py:68
  48.0 60.1 %collective-permute-start.9 = (bf16[32,1536]{1,0:T(8,128)(2,1)S(1)}, bf16[32,1536]{1,0:T(8,128)(2,1)S(1)}, u32[]{:S(2)}, u32[]{:S(2)}) collective-permute-start(bf16[32,1536]{1,0:T(8,128)(2,1)S(1)} %fusion.34), channel_id=1, source_target_pairs={{0,3},{1,0},{2,1},{3,2},{4,7},{5,4},{6,5},{7,6},{8,11},{9,8},{10,9... | collective-permute-start | bytes 294920 | tf_op jit(solution)/shard_map/ppermute | solution.py:64
  51.7 56.4 %collective-permute-start.8 = (bf16[32,1536]{1,0:T(8,128)(2,1)S(1)}, bf16[32,1536]{1,0:T(8,128)(2,1)S(1)}, u32[]{:S(2)}, u32[]{:S(2)}) collective-permute-start(bf16[32,1536]{1,0:T(8,128)(2,1)S(1)} %fusion.34), channel_id=1, source_target_pairs={{0,2},{1,3},{2,0},{3,1},{4,6},{5,7},{6,4},{7,5},{8,10},{9,11},{10,... | collective-permute-start | bytes 294920 | tf_op jit(solution)/shard_map/ppermute | solution.py:64
  51.7 56.4 %collective-permute-start.7 = (bf16[32,1536]{1,0:T(8,128)(2,1)S(1)}, bf16[32,1536]{1,0:T(8,128)(2,1)S(1)}, u32[]{:S(2)}, u32[]{:S(2)}) collective-permute-start(bf16[32,1536]{1,0:T(8,128)(2,1)S(1)} %fusion.34), channel_id=1, source_target_pairs={{0,1},{1,2},{2,3},{3,0},{4,5},{5,6},{6,7},{7,4},{8,9},{9,10},{10,1... | collective-permute-start | bytes 294920 | tf_op jit(solution)/shard_map/ppermute | solution.py:64
  85.0 1.1 copy-start.1
  101.8 5.9 %copy-start.4 = (bf16[1536,16]{0,1:T(8,128)(2,1)S(1)}, bf16[1536,16]{0,1:T(8,128)(2,1)}, u32[]{:S(2)}) copy-start(bf16[1536,16]{0,1:T(8,128)(2,1)} %param.20) | copy-start | bytes 147460
  101.8 6.1 %copy-start.5 = (s32[32,6]{0,1:T(8,128)S(1)}, s32[32,6]{0,1:T(8,128)}, u32[]{:S(2)}) copy-start(s32[32,6]{0,1:T(8,128)} %param.21) | copy-start | bytes 2308
  101.8 40.0 %all-to-all-start.1 = ((bf16[16,18,1536]{2,1,0:T(8,128)(2,1)}), bf16[16,18,1536]{2,1,0:T(8,128)(2,1)}, u32[]{:S(2)}, u32[]{:S(2)}) async-start(bf16[16,18,1536]{2,1,0:T(8,128)(2,1)} %maximum_bitcast_fusion), calls=%async_computation.1 | async-start | bytes 2359296 | tf_op jit(solution)/shard_map/all_to_all | solution.py:253
  108.1 1.1 copy-start.7
  110.2 36.1 %collective-permute-start.12 = (bf16[32,1536]{1,0:T(8,128)(2,1)}, bf16[32,1536]{1,0:T(8,128)(2,1)}, u32[]{:S(2)}, u32[]{:S(2)}) collective-permute-start(bf16[32,1536]{1,0:T(8,128)(2,1)} %get-tuple-element.12), channel_id=1, source_target_pairs={{0,1},{1,2},{2,3},{3,0},{4,5},{5,6},{6,7},{7,4},{8,9},{9,10},{10,1... | collective-permute-start | bytes 294920 | tf_op jit(solution)/shard_map/ppermute | solution.py:64
  112.1 34.2 %collective-permute-start.11 = (bf16[32,1536]{1,0:T(8,128)(2,1)}, bf16[32,1536]{1,0:T(8,128)(2,1)}, u32[]{:S(2)}, u32[]{:S(2)}) collective-permute-start(bf16[32,1536]{1,0:T(8,128)(2,1)} %get-tuple-element.13), channel_id=1, source_target_pairs={{0,2},{1,3},{2,0},{3,1},{4,6},{5,7},{6,4},{7,5},{8,10},{9,11},{10,... | collective-permute-start | bytes 294920 | tf_op jit(solution)/shard_map/ppermute | solution.py:64
  114.5 31.9 %collective-permute-start.10 = (bf16[32,1536]{1,0:T(8,128)(2,1)}, bf16[32,1536]{1,0:T(8,128)(2,1)}, u32[]{:S(2)}, u32[]{:S(2)}) collective-permute-start(bf16[32,1536]{1,0:T(8,128)(2,1)} %get-tuple-element.11), channel_id=1, source_target_pairs={{0,3},{1,0},{2,1},{3,2},{4,7},{5,4},{6,5},{7,6},{8,11},{9,8},{10,9... | collective-permute-start | bytes 294920 | tf_op jit(solution)/shard_map/ppermute | solution.py:64
where the time goes:
time: 149 us; the launch traced here: 148 us
  waiting for transfers between devices  80.2 us (54%)
  starting transfers between devices  39 us (26%)
  other arithmetic  10.2 us (7%)
  local copies, waits for them, and re-layouts  9.35 us (6%)
  matrix products  8.89 us (6%)
    all_to_all x1, waiting for transfers between devices, on_device(): lax.all_to_all(outgoing, ('ctx', 'exp'), split_axis=0, concat_axis=0, til...  26.4 us
    all_to_all x1, waiting for transfers between devices, on_device(): lax.all_to_all(result.reshape(arrived.shape), ('ctx', 'exp'), split_axis=...  25.9 us
    ppermute x3, waiting for transfers between devices, swapped(): return lax.ppermute(shard, 'group', [(0, 1), (1, 0)])  21.3 us
    ppermute x9, starting transfers between devices, turned(): lax.ppermute(shard, axis, [(i, (i + by) % length) for i in range(length)])  15.2 us
    ppermute x3, starting transfers between devices, passed_along(): return lax.ppermute(shard, axis, pairs)  11.1 us
    ppermute x9, waiting for transfers between devices, turned(): lax.ppermute(shard, axis, [(i, (i + by) % length) for i in range(length)])  6.64 us
    all_to_all x1, starting transfers between devices, on_device(): lax.all_to_all(result.reshape(arrived.shape), ('ctx', 'exp'), split_axis=...  5.92 us
    all_to_all x1, starting transfers between devices, on_device(): lax.all_to_all(outgoing, ('ctx', 'exp'), split_axis=0, concat_axis=0, til...  4.72 us
  transfers between devices with their start and end apart: 17, of which 7 were waited for; matrix products, arithmetic and copies ran while one was open for 15% of the time, Pallas kernels for 0%

commit v1 on v0

--- a/solution.py
+++ b/solution.py
@@ -6,6 +6,17 @@
 
 HEAD = 128
 neg_big = -1e30
+
+
+def flows_bring(xs, on_dim, row_data):
+    even, taken_in = (xs.shape[:on_dim], xs.shape[on_dim + 1 :])
+    return jnp.moveaxis(xs.reshape(*even, row_data, -1, *taken_in), on_dim, 0)
+
+
+def squares_push(arr, dim_at):
+    vec_out = list(arr.shape[1:])
+    vec_out[dim_at] *= arr.shape[0]
+    return jnp.moveaxis(arr, 0, dim_at).reshape(vec_out)
 
 
 def passed_along(shard, axis, by):
@@ -223,7 +234,20 @@
         down_full = lax.all_gather(expert_down, "group", axis=1, tiled=True)
     hidden_count = expert_down.shape[2]
     local_experts = expert_gate_up.shape[0]
-    arrived = lax.all_to_all(outgoing, ("ctx", "exp"), split_axis=0, concat_axis=0, tiled=True)
+
+    def _carry_surface(vals, shard_axis, inp, incoming_x=0):
+        last, all_values = (jax.lax.psum(1, shard_axis), jax.lax.axis_index(shard_axis))
+        piece_next = flows_bring(vals, inp, last)
+        history = [piece_next[all_values]]
+        for d in [*range(1, last)]:
+            reply = piece_next[all_values ^ d]
+            history.append(
+                jax.lax.ppermute(reply, shard_axis, perm=[(pp, pp ^ d) for pp in range(last)])
+            )
+        piece_next = jnp.stack(history, 0)[all_values ^ jnp.arange(last)]
+        return squares_push(piece_next, incoming_x)
+
+    arrived = _carry_surface(outgoing, ("ctx", "exp"), 0)
     sources = arrived.shape[0] // local_experts
     grouped = arrived.reshape(sources, local_experts, arrived.shape[1], arrived.shape[2])
     if swap:

time: 149 us -> 189 us (1.27)
  waiting for transfers between devices: 80.2 us -> 103 us
  local copies, waits for them, and re-layouts: 9.35 us -> 21 us
  starting transfers between devices: 39 us -> 42.8 us
  matrix products: 8.89 us -> 10.9 us
    ppermute x0 -> x15, waiting for transfers between devices: none -> 64.1 us  [_carry_surface(): jax.lax.ppermute(reply, shard_axis, perm=[(pp, pp ^ d) for pp in range(la...]
    all_to_all x1 -> x0, waiting for transfers between devices: 26.4 us -> none  [on_device(): lax.all_to_all(outgoing, ('ctx', 'exp'), split_axis=0, concat_axis=0, til...]
    ppermute x3, waiting for transfers between devices: 21.3 us -> 6.47 us  [swapped(): return lax.ppermute(shard, 'group', [(0, 1), (1, 0)])]
    ppermute x0 -> x15, starting transfers between devices: none -> 12.3 us  [_carry_surface(): jax.lax.ppermute(reply, shard_axis, perm=[(pp, pp ^ d) for pp in range(la...]
    unnamed x18 -> x32, local copies, waits for them, and re-layouts: 3.81 us -> 11.9 us
    all_to_all x1 -> x0, starting transfers between devices: 4.72 us -> none  [on_device(): lax.all_to_all(outgoing, ('ctx', 'exp'), split_axis=0, concat_axis=0, til...]
    another operation x0 -> x2, local copies, waits for them, and re-layouts: none -> 2.03 us  [the longest x1 1.4 us: flows_bring(): return jnp.moveaxis(xs.reshape(*even, row_data, -1, *taken_in), on_dim, 0)]
    gather x0 -> x1, local copies, waits for them, and re-layouts: none -> 1.89 us  [_carry_surface(): piece_next = jnp.stack(history, 0)[all_values ^ jnp.arange(last)]]
  transfers between devices with their start and end apart: 17 -> 31, of which waited for: 7 -> 19; matrix products, arithmetic and copies ran while one was open for 15% -> 20% of each run, Pallas kernels for 0% -> 0%
where the time goes in v1:
time: 189 us; the launch traced here: 188 us
  waiting for transfers between devices  103 us (54%)
  starting transfers between devices  42.8 us (23%)
  local copies, waits for them, and re-layouts  21 us (11%)
  matrix products  10.9 us (6%)
  other arithmetic  10.2 us (5%)
    ppermute x15, waiting for transfers between devices, _carry_surface(): jax.lax.ppermute(reply, shard_axis, perm=[(pp, pp ^ d) for pp in range(la...  64.1 us
    all_to_all x1, waiting for transfers between devices, on_device(): lax.all_to_all(result.reshape(arrived.shape), ('ctx', 'exp'), split_axis=...  26.5 us
    ppermute x9, starting transfers between devices, turned(): lax.ppermute(shard, axis, [(i, (i + by) % length) for i in range(length)])  13.7 us
    ppermute x15, starting transfers between devices, _carry_surface(): jax.lax.ppermute(reply, shard_axis, perm=[(pp, pp ^ d) for pp in range(la...  12.3 us
    unnamed x32, local copies, waits for them, and re-layouts  11.9 us
    ppermute x3, starting transfers between devices, passed_along(): return lax.ppermute(shard, axis, pairs)  10 us
    ppermute x3, waiting for transfers between devices, swapped(): return lax.ppermute(shard, 'group', [(0, 1), (1, 0)])  6.47 us
    ppermute x9, waiting for transfers between devices, turned(): lax.ppermute(shard, axis, [(i, (i + by) % length) for i in range(length)])  5.96 us
  transfers between devices with their start and end apart: 31, of which 19 were waited for; matrix products, arithmetic and copies ran while one was open for 20% of the time, Pallas kernels for 0%

profile of v1, /device:TPU:0, one launch (start us, length us, event | category | flops | bytes accessed | tf_op | source)
XLA Modules:
  0.0 188.5 jit_solution(13742632474757806214)
XLA Ops:
  0.9 4.3 %collective-permute-start = (bf16[2,128,128]{2,1,0:T(8,128)(2,1)S(1)}, bf16[2,128,128]{2,1,0:T(8,128)(2,1)S(1)}, u32[]{:S(2)}, u32[]{:S(2)}) collective-permute-start(bf16[2,128,128]{2,1,0:T(8,128)(2,1)S(1)} %pad_maximum_fusion.2), channel_id=1, source_target_pairs={{0,12},{4,16},{8,20},{12,24},{16,28},{1,13},{5,17},{9,21},{13,25},... | collective-permute-start | bytes 196616 | tf_op jit(solution)/shard_map/ppermute | solution.py:25
  5.2 3.3 %collective-permute-start.1 = (bf16[2,128,128]{2,1,0:T(8,128)(2,1)S(1)}, bf16[2,128,128]{2,1,0:T(8,128)(2,1)S(1)}, u32[]{:S(2)}, u32[]{:S(2)}) collective-permute-start(bf16[2,128,128]{2,1,0:T(8,128)(2,1)S(1)} %pad_maximum_fusion.2), channel_id=1, source_target_pairs={{0,8},{4,12},{8,16},{12,20},{16,24},{20,28},{1,9},{5,13},{9,17},{1... | collective-permute-start | bytes 196616 | tf_op jit(solution)/shard_map/ppermute | solution.py:25
  8.6 2.4 %collective-permute-start.2 = (bf16[2,128,128]{2,1,0:T(8,128)(2,1)S(1)}, bf16[2,128,128]{2,1,0:T(8,128)(2,1)S(1)}, u32[]{:S(2)}, u32[]{:S(2)}) collective-permute-start(bf16[2,128,128]{2,1,0:T(8,128)(2,1)S(1)} %pad_maximum_fusion.2), channel_id=1, source_target_pairs={{0,4},{4,8},{8,12},{12,16},{16,20},{20,24},{24,28},{1,5},{5,9},{9,... | collective-permute-start | bytes 196616 | tf_op jit(solution)/shard_map/ppermute | solution.py:25
  11.0 2.0 %collective-permute-start.28 = (bf16[1,768,1024]{2,1,0:T(8,128)(2,1)}, bf16[1,768,1024]{2,1,0:T(8,128)(2,1)}, u32[]{:S(2)}, u32[]{:S(2)}) collective-permute-start(bf16[1,768,1024]{2,1,0:T(8,128)(2,1)} %param.22), channel_id=1, source_target_pairs={{0,16},{16,0},{1,17},{17,1},{2,18},{18,2},{3,19},{19,3},{4,20},{20... | collective-permute-start | bytes 4718600 | tf_op jit(solution)/shard_map/ppermute | solution.py:79
  14.7 1.0 copy.31
  20.7 6.5 %collective-permute-done.3 = bf16[384,768]{1,0:T(8,128)(2,1)S(1)} collective-permute-done((bf16[384,768]{1,0:T(8,128)(2,1)}, bf16[384,768]{1,0:T(8,128)(2,1)S(1)}, u32[]{:S(2)}, u32[]{:S(2)}) %collective-permute-start.3) | collective-permute-done | bytes 589856 | tf_op jit(solution)/shard_map/ppermute | solution.py:79
  27.5 1.6 collective-permute-start.4
  29.2 2.6 %collective-permute-start.5 = (bf16[32,1536]{1,0:T(8,128)(2,1)S(1)}, bf16[32,1536]{1,0:T(8,128)(2,1)S(1)}, u32[]{:S(2)}, u32[]{:S(2)}) collective-permute-start(bf16[32,1536]{1,0:T(8,128)(2,1)S(1)} %get-tuple-element.32), channel_id=1, source_target_pairs={{0,2},{1,3},{2,0},{3,1},{4,6},{5,7},{6,4},{7,5},{8,10},{9,11},{10,... | collective-permute-start | bytes 294920 | tf_op jit(solution)/shard_map/ppermute | solution.py:75
  31.8 1.3 collective-permute-start.6
  33.1 2.0 %collective-permute-done.4 = bf16[32,1536]{1,0:T(8,128)(2,1)S(1)} collective-permute-done((bf16[32,1536]{1,0:T(8,128)(2,1)S(1)}, bf16[32,1536]{1,0:T(8,128)(2,1)S(1)}, u32[]{:S(2)}, u32[]{:S(2)}) %collective-permute-start.4) | collective-permute-done | bytes 98336 | tf_op jit(solution)/shard_map/ppermute | solution.py:75
  35.1 3.9 %collective-permute-done.5 = bf16[32,1536]{1,0:T(8,128)(2,1)S(1)} collective-permute-done((bf16[32,1536]{1,0:T(8,128)(2,1)S(1)}, bf16[32,1536]{1,0:T(8,128)(2,1)S(1)}, u32[]{:S(2)}, u32[]{:S(2)}) %collective-permute-start.5) | collective-permute-done | bytes 98336 | tf_op jit(solution)/shard_map/ppermute | solution.py:75
  39.4 1.3 convolution_convert_fusion
  40.7 1.4 reshape_reshape.3
  43.0 2.6 %collective-permute-start.13 = (bf16[1,18,1536]{2,1,0:T(8,128)(2,1)}, bf16[1,18,1536]{2,1,0:T(8,128)(2,1)S(1)}, u32[]{:S(2)}, u32[]{:S(2)}) collective-permute-start(bf16[1,18,1536]{2,1,0:T(8,128)(2,1)} %get-tuple-element.25), channel_id=1, source_target_pairs={{0,1},{1,0},{2,3},{3,2},{4,5},{5,4},{6,7},{7,6},{8,9},{9,8},{10,11... | collective-permute-start | bytes 165896 | tf_op jit(solution)/shard_map/ppermute | solution.py:245
  46.2 1.7 collective-permute-start.8
  48.5 1.5 collective-permute-start.14
  50.7 8.3 %collective-permute-done.14 = bf16[1,18,1536]{2,1,0:T(8,128)(2,1)S(1)} collective-permute-done((bf16[1,18,1536]{2,1,0:T(8,128)(2,1)}, bf16[1,18,1536]{2,1,0:T(8,128)(2,1)S(1)}, u32[]{:S(2)}, u32[]{:S(2)}) %collective-permute-start.14) | collective-permute-done | bytes 55328 | tf_op jit(solution)/shard_map/ppermute | solution.py:245
  59.1 1.7 collective-permute-start.15
  61.4 4.0 %collective-permute-done.15 = bf16[1,18,1536]{2,1,0:T(8,128)(2,1)S(1)} collective-permute-done((bf16[1,18,1536]{2,1,0:T(8,128)(2,1)}, bf16[1,18,1536]{2,1,0:T(8,128)(2,1)S(1)}, u32[]{:S(2)}, u32[]{:S(2)}) %collective-permute-start.15) | collective-permute-done | bytes 55328 | tf_op jit(solution)/shard_map/ppermute | solution.py:245
  67.5 3.8 %collective-permute-done.17 = bf16[1,18,1536]{2,1,0:T(8,128)(2,1)S(1)} collective-permute-done((bf16[1,18,1536]{2,1,0:T(8,128)(2,1)}, bf16[1,18,1536]{2,1,0:T(8,128)(2,1)S(1)}, u32[]{:S(2)}, u32[]{:S(2)}) %collective-permute-start.17) | collective-permute-done | bytes 55328 | tf_op jit(solution)/shard_map/ppermute | solution.py:245
  72.4 5.5 %collective-permute-done.18 = bf16[1,18,1536]{2,1,0:T(8,128)(2,1)S(1)} collective-permute-done((bf16[1,18,1536]{2,1,0:T(8,128)(2,1)}, bf16[1,18,1536]{2,1,0:T(8,128)(2,1)S(1)}, u32[]{:S(2)}, u32[]{:S(2)}) %collective-permute-start.18) | collective-permute-done | bytes 55328 | tf_op jit(solution)/shard_map/ppermute | solution.py:245
  77.9 1.6 collective-permute-start.19
  80.2 4.0 %collective-permute-done.19 = bf16[1,18,1536]{2,1,0:T(8,128)(2,1)S(1)} collective-permute-done((bf16[1,18,1536]{2,1,0:T(8,128)(2,1)}, bf16[1,18,1536]{2,1,0:T(8,128)(2,1)S(1)}, u32[]{:S(2)}, u32[]{:S(2)}) %collective-permute-start.19) | collective-permute-done | bytes 55328 | tf_op jit(solution)/shard_map/ppermute | solution.py:245
  84.9 3.9 %collective-permute-done.20 = bf16[1,18,1536]{2,1,0:T(8,128)(2,1)S(1)} collective-permute-done((bf16[1,18,1536]{2,1,0:T(8,128)(2,1)}, bf16[1,18,1536]{2,1,0:T(8,128)(2,1)S(1)}, u32[]{:S(2)}, u32[]{:S(2)}) %collective-permute-start.20) | collective-permute-done | bytes 55328 | tf_op jit(solution)/shard_map/ppermute | solution.py:245
  89.4 4.6 %collective-permute-done.21 = bf16[1,18,1536]{2,1,0:T(8,128)(2,1)S(1)} collective-permute-done((bf16[1,18,1536]{2,1,0:T(8,128)(2,1)S(1)}, bf16[1,18,1536]{2,1,0:T(8,128)(2,1)S(1)}, u32[]{:S(2)}, u32[]{:S(2)}) %collective-permute-start.21) | collective-permute-done | bytes 55328 | tf_op jit(solution)/shard_map/ppermute | solution.py:245
  95.1 5.8 %collective-permute-done.22 = bf16[1,18,1536]{2,1,0:T(8,128)(2,1)S(1)} collective-permute-done((bf16[1,18,1536]{2,1,0:T(8,128)(2,1)S(1)}, bf16[1,18,1536]{2,1,0:T(8,128)(2,1)S(1)}, u32[]{:S(2)}, u32[]{:S(2)}) %collective-permute-start.22) | collective-permute-done | bytes 55328 | tf_op jit(solution)/shard_map/ppermute | solution.py:245
  100.9 1.7 collective-permute-start.23
  103.3 4.7 %collective-permute-done.23 = bf16[1,18,1536]{2,1,0:T(8,128)(2,1)S(1)} collective-permute-done((bf16[1,18,1536]{2,1,0:T(8,128)(2,1)S(1)}, bf16[1,18,1536]{2,1,0:T(8,128)(2,1)S(1)}, u32[]{:S(2)}, u32[]{:S(2)}) %collective-permute-start.23) | collective-permute-done | bytes 55328 | tf_op jit(solution)/shard_map/ppermute | solution.py:245
  108.6 3.1 %collective-permute-done.24 = bf16[1,18,1536]{2,1,0:T(8,128)(2,1)S(1)} collective-permute-done((bf16[1,18,1536]{2,1,0:T(8,128)(2,1)S(1)}, bf16[1,18,1536]{2,1,0:T(8,128)(2,1)S(1)}, u32[]{:S(2)}, u32[]{:S(2)}) %collective-permute-start.24) | collective-permute-done | bytes 55328 | tf_op jit(solution)/shard_map/ppermute | solution.py:245
  112.4 4.0 %collective-permute-done.25 = bf16[1,18,1536]{2,1,0:T(8,128)(2,1)S(1)} collective-permute-done((bf16[1,18,1536]{2,1,0:T(8,128)(2,1)S(1)}, bf16[1,18,1536]{2,1,0:T(8,128)(2,1)S(1)}, u32[]{:S(2)}, u32[]{:S(2)}) %collective-permute-start.25) | collective-permute-done | bytes 55328 | tf_op jit(solution)/shard_map/ppermute | solution.py:245
  117.5 5.8 %collective-permute-done.26 = bf16[1,18,1536]{2,1,0:T(8,128)(2,1)S(1)} collective-permute-done((bf16[1,18,1536]{2,1,0:T(8,128)(2,1)S(1)}, bf16[1,18,1536]{2,1,0:T(8,128)(2,1)S(1)}, u32[]{:S(2)}, u32[]{:S(2)}) %collective-permute-start.26) | collective-permute-done | bytes 55328 | tf_op jit(solution)/shard_map/ppermute | solution.py:245
  123.3 1.7 collective-permute-start.27
  125.7 4.8 %collective-permute-done.27 = bf16[1,18,1536]{2,1,0:T(8,128)(2,1)S(1)} collective-permute-done((bf16[1,18,1536]{2,1,0:T(8,128)(2,1)S(1)}, bf16[1,18,1536]{2,1,0:T(8,128)(2,1)S(1)}, u32[]{:S(2)}, u32[]{:S(2)}) %collective-permute-start.27) | collective-permute-done | bytes 55328 | tf_op jit(solution)/shard_map/ppermute | solution.py:245
  130.5 1.8 collective-permute-start.9
  133.0 1.9 %gather_fusion = bf16[16,18,1536]{2,1,0:T(8,128)(2,1)S(1)} fusion(bf16[16,18,1536]{2,1,0:T(8,128)(2,1)} %bitcast.166, s32[1024]{0:T(1024)S(1)} %pad_clamp_fusion.1), kind=kCustom, calls=%fused_computation | custom fusion | bytes 1769536 | tf_op jit(solution)/shard_map/gather | solution.py:247
  134.9 2.2 %fusion.2 = f32[16,18,1024]{2,1,0:T(8,128)S(1)} fusion(bf16[1,768,1024]{2,1,0:T(8,128)(2,1)} %param.22, bf16[16,18,1536]{2,1,0:T(8,128)(2,1)S(1)} %gather_fusion, s32[]{:T(128)S(6)} %select_n.203), kind=kOutput, calls=%fused_computation.6 | convolution fusion | flops 452984832 | bytes 3342340 | tf_op jit(solution)/shard_map/nekd,edf->nekf/dot_general | solution.py:257
  137.1 2.2 %add_bitcast_fusion = f32[16,1,18,1024]{3,2,0,1:T(8,128)S(1)} fusion(f32[16,18,1024]{2,1,0:T(8,128)S(1)} %fusion.2, bf16[1,768,1024]{2,1,0:T(8,128)(2,1)} %collective-permute-done.28, bf16[16,18,1536]{2,1,0:T(8,128)(2,1)S(1)} %gather_fusion, s32[]{:T(128)S(6)} %select_n.204), kind=kOutput, calls=%fused_computation.11 | convolution fusion | flops 453279744 | bytes 4915204 | tf_op jit(solution)/shard_map/nekd,edf->nekf/dot_general | solution.py:259
  141.0 1.6 select_bitcast_fusion.1
  142.6 1.1 maximum_bitcast_fusion
  143.7 4.5 %all-to-all-start = ((bf16[16,18,1536]{2,1,0:T(8,128)(2,1)}), bf16[16,18,1536]{2,1,0:T(8,128)(2,1)}, u32[]{:S(2)}, u32[]{:S(2)}) async-start(bf16[16,18,1536]{2,1,0:T(8,128)(2,1)} %maximum_bitcast_fusion), calls=%async_computation | async-start | bytes 2359296 | tf_op jit(solution)/shard_map/all_to_all | solution.py:277
  148.6 1.4 fusion.4
  151.0 3.6 %collective-permute-start.10 = (bf16[32,1536]{1,0:T(8,128)(2,1)}, bf16[32,1536]{1,0:T(8,128)(2,1)}, u32[]{:S(2)}, u32[]{:S(2)}) collective-permute-start(bf16[32,1536]{1,0:T(8,128)(2,1)} %get-tuple-element.27), channel_id=1, source_target_pairs={{0,3},{1,0},{2,1},{3,2},{4,7},{5,4},{6,5},{7,6},{8,11},{9,8},{10,9... | collective-permute-start | bytes 294920 | tf_op jit(solution)/shard_map/ppermute | solution.py:75
  154.6 1.1 collective-permute-start.12
  155.7 26.5 %all-to-all-done = bf16[16,18,1536]{2,1,0:T(8,128)(2,1)} async-done(((bf16[16,18,1536]{2,1,0:T(8,128)(2,1)}), bf16[16,18,1536]{2,1,0:T(8,128)(2,1)}, u32[]{:S(2)}, u32[]{:S(2)}) %all-to-all-start) | async-done | bytes 884768 | tf_op jit(solution)/shard_map/all_to_all | solution.py:277
  182.2 1.5 reshape.210
  183.7 1.2 gather_fusion.1
  185.2 1.6 multiply_reduce_fusion
  186.8 1.7 fusion.36
  (100 shorter events, 25.0 us)
Async XLA Ops:
  0.0 148.6 %copy-start = (bf16[1536,2,256]{2,1,0:T(2,128)(2,1)S(1)}, bf16[1536,2,256]{2,1,0:T(2,128)(2,1)}, u32[]{:S(2)}) copy-start(bf16[1536,2,256]{2,1,0:T(2,128)(2,1)} %param.24) | copy-start | bytes 4718596
  0.9 17.0 %collective-permute-start = (bf16[2,128,128]{2,1,0:T(8,128)(2,1)S(1)}, bf16[2,128,128]{2,1,0:T(8,128)(2,1)S(1)}, u32[]{:S(2)}, u32[]{:S(2)}) collective-permute-start(bf16[2,128,128]{2,1,0:T(8,128)(2,1)S(1)} %pad_maximum_fusion.2), channel_id=1, source_target_pairs={{0,12},{4,16},{8,20},{12,24},{16,28},{1,13},{5,17},{9,21},{13,25},... | collective-permute-start | bytes 196616 | tf_op jit(solution)/shard_map/ppermute | solution.py:25
  5.2 12.9 %collective-permute-start.1 = (bf16[2,128,128]{2,1,0:T(8,128)(2,1)S(1)}, bf16[2,128,128]{2,1,0:T(8,128)(2,1)S(1)}, u32[]{:S(2)}, u32[]{:S(2)}) collective-permute-start(bf16[2,128,128]{2,1,0:T(8,128)(2,1)S(1)} %pad_maximum_fusion.2), channel_id=1, source_target_pairs={{0,8},{4,12},{8,16},{12,20},{16,24},{20,28},{1,9},{5,13},{9,17},{1... | collective-permute-start | bytes 196616 | tf_op jit(solution)/shard_map/ppermute | solution.py:25
  8.6 9.5 %collective-permute-start.2 = (bf16[2,128,128]{2,1,0:T(8,128)(2,1)S(1)}, bf16[2,128,128]{2,1,0:T(8,128)(2,1)S(1)}, u32[]{:S(2)}, u32[]{:S(2)}) collective-permute-start(bf16[2,128,128]{2,1,0:T(8,128)(2,1)S(1)} %pad_maximum_fusion.2), channel_id=1, source_target_pairs={{0,4},{4,8},{8,12},{12,16},{16,20},{20,24},{24,28},{1,5},{5,9},{9,... | collective-permute-start | bytes 196616 | tf_op jit(solution)/shard_map/ppermute | solution.py:25
  10.9 16.3 %collective-permute-start.3 = (bf16[384,768]{1,0:T(8,128)(2,1)}, bf16[384,768]{1,0:T(8,128)(2,1)S(1)}, u32[]{:S(2)}, u32[]{:S(2)}) collective-permute-start(bf16[384,768]{1,0:T(8,128)(2,1)} %param.18), channel_id=1, source_target_pairs={{0,16},{16,0},{1,17},{17,1},{2,18},{18,2},{3,19},{19,3},{4,20},{20... | collective-permute-start | bytes 1769480 | tf_op jit(solution)/shard_map/ppermute | solution.py:79
  11.0 126.1 %collective-permute-start.28 = (bf16[1,768,1024]{2,1,0:T(8,128)(2,1)}, bf16[1,768,1024]{2,1,0:T(8,128)(2,1)}, u32[]{:S(2)}, u32[]{:S(2)}) collective-permute-start(bf16[1,768,1024]{2,1,0:T(8,128)(2,1)} %param.22), channel_id=1, source_target_pairs={{0,16},{16,0},{1,17},{17,1},{2,18},{18,2},{3,19},{19,3},{4,20},{20... | collective-permute-start | bytes 4718600 | tf_op jit(solution)/shard_map/ppermute | solution.py:79
  18.0 123.0 %collective-permute-start.29 = (bf16[1,768,512]{2,1,0:T(8,128)(2,1)}, bf16[1,768,512]{2,1,0:T(8,128)(2,1)}, u32[]{:S(2)}, u32[]{:S(2)}) collective-permute-start(bf16[1,768,512]{2,1,0:T(8,128)(2,1)} %param.23), channel_id=1, source_target_pairs={{0,16},{16,0},{1,17},{17,1},{2,18},{18,2},{3,19},{19,3},{4,20},{20... | collective-permute-start | bytes 2359304 | tf_op jit(solution)/shard_map/ppermute | solution.py:79
  19.3 1.1 copy-start.2
  20.7 18.4 %copy-start.3 = (bf16[32,1536]{1,0:T(8,128)(2,1)S(1)}, bf16[32,1536]{1,0:T(8,128)(2,1)}, u32[]{:S(2)}) copy-start(bf16[32,1536]{1,0:T(8,128)(2,1)} %param.16) | copy-start | bytes 294916
  20.7 18.5 %copy-start.6 = (f32[1536]{0:T(1024)S(1)}, f32[1536]{0:T(1024)}, u32[]{:S(2)}) copy-start(f32[1536]{0:T(1024)} %param.19) | copy-start | bytes 18436
  27.5 7.6 %collective-permute-start.4 = (bf16[32,1536]{1,0:T(8,128)(2,1)S(1)}, bf16[32,1536]{1,0:T(8,128)(2,1)S(1)}, u32[]{:S(2)}, u32[]{:S(2)}) collective-permute-start(bf16[32,1536]{1,0:T(8,128)(2,1)S(1)} %get-tuple-element.30), channel_id=1, source_target_pairs={{0,1},{1,2},{2,3},{3,0},{4,5},{5,6},{6,7},{7,4},{8,9},{9,10},{10,1... | collective-permute-start | bytes 294920 | tf_op jit(solution)/shard_map/ppermute | solution.py:75
  29.2 9.9 %collective-permute-start.5 = (bf16[32,1536]{1,0:T(8,128)(2,1)S(1)}, bf16[32,1536]{1,0:T(8,128)(2,1)S(1)}, u32[]{:S(2)}, u32[]{:S(2)}) collective-permute-start(bf16[32,1536]{1,0:T(8,128)(2,1)S(1)} %get-tuple-element.32), channel_id=1, source_target_pairs={{0,2},{1,3},{2,0},{3,1},{4,6},{5,7},{6,4},{7,5},{8,10},{9,11},{10,... | collective-permute-start | bytes 294920 | tf_op jit(solution)/shard_map/ppermute | solution.py:75
  31.8 7.3 %collective-permute-start.6 = (bf16[32,1536]{1,0:T(8,128)(2,1)S(1)}, bf16[32,1536]{1,0:T(8,128)(2,1)S(1)}, u32[]{:S(2)}, u32[]{:S(2)}) collective-permute-start(bf16[32,1536]{1,0:T(8,128)(2,1)S(1)} %get-tuple-element.31), channel_id=1, source_target_pairs={{0,3},{1,0},{2,1},{3,2},{4,7},{5,4},{6,5},{7,6},{8,11},{9,8},{10,9... | collective-permute-start | bytes 294920 | tf_op jit(solution)/shard_map/ppermute | solution.py:75
  43.0 5.6 %collective-permute-start.13 = (bf16[1,18,1536]{2,1,0:T(8,128)(2,1)}, bf16[1,18,1536]{2,1,0:T(8,128)(2,1)S(1)}, u32[]{:S(2)}, u32[]{:S(2)}) collective-permute-start(bf16[1,18,1536]{2,1,0:T(8,128)(2,1)} %get-tuple-element.25), channel_id=1, source_target_pairs={{0,1},{1,0},{2,3},{3,2},{4,5},{5,4},{6,7},{7,6},{8,9},{9,8},{10,11... | collective-permute-start | bytes 165896 | tf_op jit(solution)/shard_map/ppermute | solution.py:245
  46.2 102.4 %collective-permute-start.7 = (bf16[32,1536]{1,0:T(8,128)(2,1)S(1)}, bf16[32,1536]{1,0:T(8,128)(2,1)}, u32[]{:S(2)}, u32[]{:S(2)}) collective-permute-start(bf16[32,1536]{1,0:T(8,128)(2,1)S(1)} %fusion.34), channel_id=1, source_target_pairs={{0,1},{1,2},{2,3},{3,0},{4,5},{5,6},{6,7},{7,4},{8,9},{9,10},{10,1... | collective-permute-start | bytes 294920 | tf_op jit(solution)/shard_map/ppermute | solution.py:75
  46.2 102.4 %collective-permute-start.8 = (bf16[32,1536]{1,0:T(8,128)(2,1)S(1)}, bf16[32,1536]{1,0:T(8,128)(2,1)}, u32[]{:S(2)}, u32[]{:S(2)}) collective-permute-start(bf16[32,1536]{1,0:T(8,128)(2,1)S(1)} %fusion.34), channel_id=1, source_target_pairs={{0,2},{1,3},{2,0},{3,1},{4,6},{5,7},{6,4},{7,5},{8,10},{9,11},{10,... | collective-permute-start | bytes 294920 | tf_op jit(solution)/shard_map/ppermute | solution.py:75
  48.5 10.5 %collective-permute-start.14 = (bf16[1,18,1536]{2,1,0:T(8,128)(2,1)}, bf16[1,18,1536]{2,1,0:T(8,128)(2,1)S(1)}, u32[]{:S(2)}, u32[]{:S(2)}) collective-permute-start(bf16[1,18,1536]{2,1,0:T(8,128)(2,1)} %get-tuple-element.24), channel_id=1, source_target_pairs={{0,2},{1,3},{2,0},{3,1},{4,6},{5,7},{6,4},{7,5},{8,10},{9,11},{10,... | collective-permute-start | bytes 165896 | tf_op jit(solution)/shard_map/ppermute | solution.py:245
  59.1 6.4 %collective-permute-start.15 = (bf16[1,18,1536]{2,1,0:T(8,128)(2,1)}, bf16[1,18,1536]{2,1,0:T(8,128)(2,1)S(1)}, u32[]{:S(2)}, u32[]{:S(2)}) collective-permute-start(bf16[1,18,1536]{2,1,0:T(8,128)(2,1)} %get-tuple-element.23), channel_id=1, source_target_pairs={{0,3},{1,2},{2,1},{3,0},{4,7},{5,6},{6,5},{7,4},{8,11},{9,10},{10,... | collective-permute-start | bytes 165896 | tf_op jit(solution)/shard_map/ppermute | solution.py:245
  65.4 1.5 collective-permute-start.16
  66.9 4.4 %collective-permute-start.17 = (bf16[1,18,1536]{2,1,0:T(8,128)(2,1)}, bf16[1,18,1536]{2,1,0:T(8,128)(2,1)S(1)}, u32[]{:S(2)}, u32[]{:S(2)}) collective-permute-start(bf16[1,18,1536]{2,1,0:T(8,128)(2,1)} %get-tuple-element.21), channel_id=1, source_target_pairs={{0,5},{1,4},{2,7},{3,6},{4,1},{5,0},{6,3},{7,2},{8,13},{9,12},{10,... | collective-permute-start | bytes 165896 | tf_op jit(solution)/shard_map/ppermute | solution.py:245
  71.3 6.6 %collective-permute-start.18 = (bf16[1,18,1536]{2,1,0:T(8,128)(2,1)}, bf16[1,18,1536]{2,1,0:T(8,128)(2,1)S(1)}, u32[]{:S(2)}, u32[]{:S(2)}) collective-permute-start(bf16[1,18,1536]{2,1,0:T(8,128)(2,1)} %get-tuple-element.20), channel_id=1, source_target_pairs={{0,6},{1,7},{2,4},{3,5},{4,2},{5,3},{6,0},{7,1},{8,14},{9,15},{10,... | collective-permute-start | bytes 165896 | tf_op jit(solution)/shard_map/ppermute | solution.py:245
  77.9 6.3 %collective-permute-start.19 = (bf16[1,18,1536]{2,1,0:T(8,128)(2,1)}, bf16[1,18,1536]{2,1,0:T(8,128)(2,1)S(1)}, u32[]{:S(2)}, u32[]{:S(2)}) collective-permute-start(bf16[1,18,1536]{2,1,0:T(8,128)(2,1)} %get-tuple-element.19), channel_id=1, source_target_pairs={{0,7},{1,6},{2,5},{3,4},{4,3},{5,2},{6,1},{7,0},{8,15},{9,14},{10,... | collective-permute-start | bytes 165896 | tf_op jit(solution)/shard_map/ppermute | solution.py:245
  84.2 4.6 %collective-permute-start.20 = (bf16[1,18,1536]{2,1,0:T(8,128)(2,1)}, bf16[1,18,1536]{2,1,0:T(8,128)(2,1)S(1)}, u32[]{:S(2)}, u32[]{:S(2)}) collective-permute-start(bf16[1,18,1536]{2,1,0:T(8,128)(2,1)} %get-tuple-element.18), channel_id=1, source_target_pairs={{0,8},{1,9},{2,10},{3,11},{4,12},{5,13},{6,14},{7,15},{8,0},{9,1},... | collective-permute-start | bytes 165896 | tf_op jit(solution)/shard_map/ppermute | solution.py:245
  88.8 5.3 %collective-permute-start.21 = (bf16[1,18,1536]{2,1,0:T(8,128)(2,1)S(1)}, bf16[1,18,1536]{2,1,0:T(8,128)(2,1)S(1)}, u32[]{:S(2)}, u32[]{:S(2)}) collective-permute-start(bf16[1,18,1536]{2,1,0:T(8,128)(2,1)S(1)} %get-tuple-element.17), channel_id=1, source_target_pairs={{0,9},{1,8},{2,11},{3,10},{4,13},{5,12},{6,15},{7,14},{8,1},{9,0},... | collective-permute-start | bytes 165896 | tf_op jit(solution)/shard_map/ppermute | solution.py:245
  94.0 6.9 %collective-permute-start.22 = (bf16[1,18,1536]{2,1,0:T(8,128)(2,1)S(1)}, bf16[1,18,1536]{2,1,0:T(8,128)(2,1)S(1)}, u32[]{:S(2)}, u32[]{:S(2)}) collective-permute-start(bf16[1,18,1536]{2,1,0:T(8,128)(2,1)S(1)} %get-tuple-element.16), channel_id=1, source_target_pairs={{0,10},{1,11},{2,8},{3,9},{4,14},{5,15},{6,12},{7,13},{8,2},{9,3},... | collective-permute-start | bytes 165896 | tf_op jit(solution)/shard_map/ppermute | solution.py:245
  100.9 7.0 %collective-permute-start.23 = (bf16[1,18,1536]{2,1,0:T(8,128)(2,1)S(1)}, bf16[1,18,1536]{2,1,0:T(8,128)(2,1)S(1)}, u32[]{:S(2)}, u32[]{:S(2)}) collective-permute-start(bf16[1,18,1536]{2,1,0:T(8,128)(2,1)S(1)} %get-tuple-element.15), channel_id=1, source_target_pairs={{0,11},{1,10},{2,9},{3,8},{4,15},{5,14},{6,13},{7,12},{8,3},{9,2},... | collective-permute-start | bytes 165896 | tf_op jit(solution)/shard_map/ppermute | solution.py:245
  108.0 3.8 %collective-permute-start.24 = (bf16[1,18,1536]{2,1,0:T(8,128)(2,1)S(1)}, bf16[1,18,1536]{2,1,0:T(8,128)(2,1)S(1)}, u32[]{:S(2)}, u32[]{:S(2)}) collective-permute-start(bf16[1,18,1536]{2,1,0:T(8,128)(2,1)S(1)} %get-tuple-element.14), channel_id=1, source_target_pairs={{0,12},{1,13},{2,14},{3,15},{4,8},{5,9},{6,10},{7,11},{8,4},{9,5},... | collective-permute-start | bytes 165896 | tf_op jit(solution)/shard_map/ppermute | solution.py:245
  111.8 4.7 %collective-permute-start.25 = (bf16[1,18,1536]{2,1,0:T(8,128)(2,1)S(1)}, bf16[1,18,1536]{2,1,0:T(8,128)(2,1)S(1)}, u32[]{:S(2)}, u32[]{:S(2)}) collective-permute-start(bf16[1,18,1536]{2,1,0:T(8,128)(2,1)S(1)} %get-tuple-element.13), channel_id=1, source_target_pairs={{0,13},{1,12},{2,15},{3,14},{4,9},{5,8},{6,11},{7,10},{8,5},{9,4},... | collective-permute-start | bytes 165896 | tf_op jit(solution)/shard_map/ppermute | solution.py:245
  116.4 6.9 %collective-permute-start.26 = (bf16[1,18,1536]{2,1,0:T(8,128)(2,1)S(1)}, bf16[1,18,1536]{2,1,0:T(8,128)(2,1)S(1)}, u32[]{:S(2)}, u32[]{:S(2)}) collective-permute-start(bf16[1,18,1536]{2,1,0:T(8,128)(2,1)S(1)} %get-tuple-element.12), channel_id=1, source_target_pairs={{0,14},{1,15},{2,12},{3,13},{4,10},{5,11},{6,8},{7,9},{8,6},{9,7},... | collective-permute-start | bytes 165896 | tf_op jit(solution)/shard_map/ppermute | solution.py:245
  123.3 7.2 %collective-permute-start.27 = (bf16[1,18,1536]{2,1,0:T(8,128)(2,1)S(1)}, bf16[1,18,1536]{2,1,0:T(8,128)(2,1)S(1)}, u32[]{:S(2)}, u32[]{:S(2)}) collective-permute-start(bf16[1,18,1536]{2,1,0:T(8,128)(2,1)S(1)} %get-tuple-element.11), channel_id=1, source_target_pairs={{0,15},{1,14},{2,13},{3,12},{4,11},{5,10},{6,9},{7,8},{8,7},{9,6},... | collective-permute-start | bytes 165896 | tf_op jit(solution)/shard_map/ppermute | solution.py:245
  130.5 18.1 %collective-permute-start.9 = (bf16[32,1536]{1,0:T(8,128)(2,1)S(1)}, bf16[32,1536]{1,0:T(8,128)(2,1)S(1)}, u32[]{:S(2)}, u32[]{:S(2)}) collective-permute-start(bf16[32,1536]{1,0:T(8,128)(2,1)S(1)} %fusion.34), channel_id=1, source_target_pairs={{0,3},{1,0},{2,1},{3,2},{4,7},{5,4},{6,5},{7,6},{8,11},{9,8},{10,9... | collective-permute-start | bytes 294920 | tf_op jit(solution)/shard_map/ppermute | solution.py:75
  139.3 1.1 copy-start.1
  143.7 4.5 %copy-start.4 = (bf16[1536,16]{0,1:T(8,128)(2,1)S(1)}, bf16[1536,16]{0,1:T(8,128)(2,1)}, u32[]{:S(2)}) copy-start(bf16[1536,16]{0,1:T(8,128)(2,1)} %param.20) | copy-start | bytes 147460
  143.7 4.7 %copy-start.5 = (s32[32,6]{0,1:T(8,128)S(1)}, s32[32,6]{0,1:T(8,128)}, u32[]{:S(2)}) copy-start(s32[32,6]{0,1:T(8,128)} %param.21) | copy-start | bytes 2308
  143.7 38.5 %all-to-all-start = ((bf16[16,18,1536]{2,1,0:T(8,128)(2,1)}), bf16[16,18,1536]{2,1,0:T(8,128)(2,1)}, u32[]{:S(2)}, u32[]{:S(2)}) async-start(bf16[16,18,1536]{2,1,0:T(8,128)(2,1)} %maximum_bitcast_fusion), calls=%async_computation | async-start | bytes 2359296 | tf_op jit(solution)/shard_map/all_to_all | solution.py:277
  148.6 1.4 copy-start.7
  151.0 35.7 %collective-permute-start.10 = (bf16[32,1536]{1,0:T(8,128)(2,1)}, bf16[32,1536]{1,0:T(8,128)(2,1)}, u32[]{:S(2)}, u32[]{:S(2)}) collective-permute-start(bf16[32,1536]{1,0:T(8,128)(2,1)} %get-tuple-element.27), channel_id=1, source_target_pairs={{0,3},{1,0},{2,1},{3,2},{4,7},{5,4},{6,5},{7,6},{8,11},{9,8},{10,9... | collective-permute-start | bytes 294920 | tf_op jit(solution)/shard_map/ppermute | solution.py:75
  154.6 32.2 %collective-permute-start.11 = (bf16[32,1536]{1,0:T(8,128)(2,1)}, bf16[32,1536]{1,0:T(8,128)(2,1)}, u32[]{:S(2)}, u32[]{:S(2)}) collective-permute-start(bf16[32,1536]{1,0:T(8,128)(2,1)} %get-tuple-element.29), channel_id=1, source_target_pairs={{0,2},{1,3},{2,0},{3,1},{4,6},{5,7},{6,4},{7,5},{8,10},{9,11},{10,... | collective-permute-start | bytes 294920 | tf_op jit(solution)/shard_map/ppermute | solution.py:75
  154.6 32.2 %collective-permute-start.12 = (bf16[32,1536]{1,0:T(8,128)(2,1)}, bf16[32,1536]{1,0:T(8,128)(2,1)}, u32[]{:S(2)}, u32[]{:S(2)}) collective-permute-start(bf16[32,1536]{1,0:T(8,128)(2,1)} %get-tuple-element.28), channel_id=1, source_target_pairs={{0,1},{1,2},{2,3},{3,0},{4,5},{5,6},{6,7},{7,4},{8,9},{9,10},{10,1... | collective-permute-start | bytes 294920 | tf_op jit(solution)/shard_map/ppermute | solution.py:75
